TPU v7x, 128 devices: a whole 4x4x4 slice. The times are simulated.
128 devices in a mesh: shard: 16 (over y, x), sub: 8 (over z, core).
Axes of the slice: x: 4, y: 4, z: 4, core: 2. Of those that a mesh axis runs over, the one named last changes fastest.
Arguments:
- queries: bfloat16 [256, 2048], P(('shard', 'sub')), may hold values from -128 to 128
- passages: bfloat16 [262144, 2048], P(('shard', 'sub')), may hold values from -32 to 32
- candidates: int32 [256, 200], P(('shard', 'sub')), may hold values from 0 to 262143, as said below
Outputs:
- coarse_lse: float32 [256], P(('shard', 'sub'))
- cand_probs: float32 [256, 200], P(('shard', 'sub'))
- pooled: bfloat16 [256, 2048], P(('shard', 'sub'))
Inputs may be any that keep to these rules, and one draw needn't show every extreme that they name: Every id names a passage. Among the 200 candidates of the 2 queries owned by one device (aligned blocks of rows), at most 8 name passages held by one device (id // 2048); in every block at least two owners are named exactly 8 times, one of them the same owner for every block.
All inputs are finite; a program needn't handle non-finite values.
Results may differ from a plain program's by a relative error of at most 0.0025.
The roundings to bfloat16 on the way count: a program that leaves them out, or rounds other values in their place, can miss the bound.
Values may be sent and summed in bfloat16 or wider, within the bound.
A program may use at most 64 MiB of HBM per device.

v0:
```python
import jax
import jax.numpy as jnp
from jax import lax
from jax.sharding import PartitionSpec as P

PREFIX = 64


def combined_all(value, axis, join):
    pieces = lax.all_gather(value, axis)
    head = pieces[0]
    tail = pieces[1:]
    so_far, _ = lax.scan(lambda so_far, section: (join(so_far, section), None), head, tail)
    return so_far


def joined(left_lse, right_lse):
    highest = jnp.maximum(left_lse, right_lse)
    return highest + jnp.log(jnp.exp(left_lse - highest) + jnp.exp(right_lse - highest))


def shards(queries, passages, candidates):
    qry_dev, width = queries.shape
    pas_dev = passages.shape[0]
    devices = lax.axis_size(("shard", "sub"))
    prefix_rows = passages[:, :PREFIX]
    scores = jnp.dot(
        lax.all_gather(queries[:, :PREFIX], ("shard", "sub"), axis=0, tiled=True),
        prefix_rows.T,
        preferred_element_type=jnp.float32,
    ) * PREFIX ** (-0.5)
    highest = jnp.max(scores, axis=1)
    local_lse = highest + jnp.log(jnp.sum(jnp.exp(scores - highest[:, None]), axis=1))
    every_lse = combined_all(local_lse, ("shard", "sub"), joined)
    coarse_lse = lax.dynamic_slice_in_dim(
        every_lse, lax.axis_index(("shard", "sub")) * qry_dev, qry_dev, 0
    )
    cands = candidates.shape[1]
    flat_ids = candidates.reshape(-1)
    needed = flat_ids.shape[0]
    capacity = ((3 * needed + 2 * devices - 1) // (2 * devices) + 7) // 8 * 8
    owners = flat_ids // pas_dev
    local_ids = flat_ids % pas_dev
    onehot = (owners[:, None] == jnp.arange(devices, dtype=jnp.int32)[None, :]).astype(jnp.int32)
    running = jnp.cumsum(onehot, axis=0)
    slot_ids = jnp.sum(running * onehot, axis=1) - 1
    request = jnp.zeros((devices, capacity), jnp.int32).at[owners, slot_ids].set(local_ids)
    incoming = lax.all_to_all(request, ("shard", "sub"), split_axis=0, concat_axis=0, tiled=True)
    fetched = jnp.take(passages, incoming.reshape(-1), axis=0).reshape(devices, capacity, width)
    returned = lax.all_to_all(fetched, ("shard", "sub"), split_axis=0, concat_axis=0, tiled=True)
    cand_rows = returned[owners, slot_ids].reshape(qry_dev, cands, width)
    scores = jnp.einsum(
        "qd,qcd->qc", queries, cand_rows, preferred_element_type=jnp.float32
    ) * width ** (-0.5)
    cand_probs = jax.nn.softmax(scores, axis=1)
    cand_weights = cand_probs.astype(jnp.bfloat16)
    pooled = jnp.einsum("qc,qcd->qd", cand_weights, cand_rows, preferred_element_type=jnp.float32)
    return (coarse_lse, cand_probs, pooled.astype(jnp.bfloat16))


def solution(mesh):
    in_specs = (P(("shard", "sub"), None), P(("shard", "sub"), None), P(("shard", "sub"), None))
    out_specs = (P(("shard", "sub")), P(("shard", "sub"), None), P(("shard", "sub"), None))
    return jax.shard_map(shards, mesh=mesh, in_specs=in_specs, out_specs=out_specs, check_vma=False)
```

profile of v0, /device:TPU:0, one launch (start us, length us, event | category | flops | bytes accessed | tf_op | source)
XLA Modules:
  0.0 194.0 jit_solution(3932196441076820813)
XLA Ops:
  0.6 0.8 reshape.203
  1.4 0.8 reshape.202
  2.2 0.1 iota_compare_fusion
  2.3 0.2 fusion.2
  2.6 0.2 fusion.4
  2.9 0.0 copy-start.1
  2.9 18.7 %scatter_fusion = s32[128,8]{0,1:T(8,128)S(1)} fusion(s32[128,8]{0,1:T(8,128)S(1)} %broadcast_in_dim.12, s32[400]{0:T(512)S(1)} %bitcast.52, s32[400]{0:T(512)S(1)} %get-tuple-element.31), kind=kCustom, calls=%fused_computation.2 | custom fusion | bytes 8000 | tf_op jit(solution)/shard_map/scatter | solution.py:47
  21.6 0.7 copy.13
  22.3 11.1 %all-to-all-start = ((s32[128,1,8]{2,1,0:T(1,128)}), s32[128,1,8]{2,1,0:T(1,128)S(1)}, u32[]{:S(2)}, u32[]{:S(2)}) async-start(s32[128,1,8]{2,1,0:T(1,128)} %copy.13), calls=%async_computation | async-start | bytes 131072 | tf_op jit(solution)/shard_map/all_to_all | solution.py:48
  33.5 0.0 copy-done.1
  33.5 31.7 %all-gather.1 = bf16[128,2,64]{2,1,0:T(2,128)(2,1)S(1)} all-gather(bf16[1,2,64]{2,1,0:T(2,128)(2,1)S(1)} %slice_bitcast_fusion.1), channel_id=1, replica_groups=mesh['shard'=16,'sub'=8] {'shard','sub'}, dimensions={0}, use_global_device_ids=true | all-gather | bytes 33024 | tf_op jit(solution)/shard_map/all_gather | solution.py:28
  65.2 1.6 fusion.16
  66.8 0.4 exponential_reduce_fusion
  67.2 33.0 %all-gather.2 = f32[128,1,256]{2,1,0:T(1,128)S(1)} all-gather(f32[1,1,256]{2,1,0:T(1,128)S(1)} %bitcast.70), channel_id=2, replica_groups=mesh['shard'=16,'sub'=8] {'shard','sub'}, dimensions={0}, use_global_device_ids=true | all-gather | bytes 132096 | tf_op jit(solution)/shard_map/all_gather | solution.py:10
  100.2 0.0 copy-start
  100.2 0.0 all-to-all-done
  100.2 0.5 broadcast.245
  100.8 0.8 reduce.3
  101.6 0.1 reshape.207
  101.7 13.3 %gather_fusion = bf16[1024,2048]{1,0:T(8,128)(2,1)} fusion(bf16[2048,2048]{1,0:T(8,128)(2,1)} %param.6, s32[1024]{0:T(1024)S(1)} %broadcast_clamp_fusion), kind=kCustom, calls=%fused_computation | custom fusion | bytes 8392704 | tf_op jit(solution)/shard_map/jit(_take)/gather | solution.py:49
  115.0 0.0 copy-done
  115.1 0.1 copy.15
  115.2 4.6 %bitcast_select_fusion = bf16[128,8,2048]{2,1,0:T(8,128)(2,1)} fusion(bf16[1024,2048]{1,0:T(8,128)(2,1)} %gather_fusion, pred[128,8]{1,0:T(8,128)(4,1)S(1)} %copy.15), kind=kLoop, calls=%fused_computation.7 | loop fusion | flops 2097152 | bytes 8389632 | tf_op jit(solution)/shard_map/jit(_take)/select_n | solution.py:49
  119.8 0.0 slice-start
  119.8 6.8 %all-to-all-start.1 = ((bf16[128,8,2048]{2,1,0:T(8,128)(2,1)}), bf16[128,8,2048]{2,1,0:T(8,128)(2,1)}, u32[]{:S(2)}, u32[]{:S(2)}) async-start(bf16[128,8,2048]{2,1,0:T(8,128)(2,1)} %bitcast_select_fusion), calls=%async_computation.1 | async-start | bytes 8388608 | tf_op jit(solution)/shard_map/all_to_all | solution.py:50
  126.6 0.0 slice-done
  126.6 6.4 %while.10 = (s32[]{:T(128)}, f32[256]{0:T(256)S(1)}, f32[127,256]{1,0:T(8,128)S(1)}, s32[]{:T(128)}) while((s32[]{:T(128)}, f32[256]{0:T(256)S(1)}, f32[127,256]{1,0:T(8,128)S(1)}, s32[]{:T(128)}) %tuple.31), condition=%wide.region_3.4_spmd, body=%wide.region_2.3_spmd.sunk | while | flops 1282 | bytes 5177 | solution.py:13
  133.1 0.6 dynamic_slice.7
  133.6 45.3 %all-to-all-done.1 = bf16[128,8,2048]{2,1,0:T(8,128)(2,1)} async-done(((bf16[128,8,2048]{2,1,0:T(8,128)(2,1)}), bf16[128,8,2048]{2,1,0:T(8,128)(2,1)}, u32[]{:S(2)}, u32[]{:S(2)}) %all-to-all-start.1) | async-done | bytes 4194336 | tf_op jit(solution)/shard_map/all_to_all | solution.py:50
  178.9 12.5 %gather_fusion.1 = bf16[400,2048]{1,0:T(8,128)(2,1)S(1)} fusion(bf16[128,8,2048]{2,1,0:T(8,128)(2,1)} %all-to-all-done.1, s32[400]{0:T(512)S(1)} %bitcast.53), kind=kCustom, calls=%fused_computation.1 | custom fusion | bytes 3280000 | tf_op jit(solution)/shard_map/gather | solution.py:51
  191.5 0.5 fusion.5
  192.0 0.1 fusion.13
  192.1 0.2 fusion.12
  192.3 0.7 convert_bitcast_fusion
  193.0 0.4 fusion.8
  193.4 0.6 copy.38
  (273 shorter events, 3.9 us)
Async XLA Ops:
  2.9 30.6 %copy-start.1 = (bf16[2,2048]{1,0:T(2,128)(2,1)S(1)}, bf16[2,2048]{1,0:T(2,128)(2,1)}, u32[]{:S(2)}) copy-start(bf16[2,2048]{1,0:T(2,128)(2,1)} %param.5) | copy-start | bytes 24580
  22.3 77.9 %all-to-all-start = ((s32[128,1,8]{2,1,0:T(1,128)}), s32[128,1,8]{2,1,0:T(1,128)S(1)}, u32[]{:S(2)}, u32[]{:S(2)}) async-start(s32[128,1,8]{2,1,0:T(1,128)} %copy.13), calls=%async_computation | async-start | bytes 131072 | tf_op jit(solution)/shard_map/all_to_all | solution.py:48
  100.2 14.8 %copy-start = (f32[128,1,256]{2,1,0:T(1,128)}, f32[128,1,256]{2,1,0:T(1,128)S(1)}, u32[]{:S(2)}) copy-start(f32[128,1,256]{2,1,0:T(1,128)S(1)} %all-gather.2) | copy-start | bytes 393220
  119.8 6.8 %slice-start = ((f32[128,1,256]{2,1,0:T(1,128)}), f32[1,1,256]{2,1,0:T(1,128)S(1)}, s32[]{:S(2)}) async-start(f32[128,1,256]{2,1,0:T(1,128)} %copy-done), calls=%async_computation.2 | async-start | bytes 2048 | tf_op jit(solution)/shard_map/slice | solution.py:11
  119.8 59.2 %all-to-all-start.1 = ((bf16[128,8,2048]{2,1,0:T(8,128)(2,1)}), bf16[128,8,2048]{2,1,0:T(8,128)(2,1)}, u32[]{:S(2)}, u32[]{:S(2)}) async-start(bf16[128,8,2048]{2,1,0:T(8,128)(2,1)} %bitcast_select_fusion), calls=%async_computation.1 | async-start | bytes 8388608 | tf_op jit(solution)/shard_map/all_to_all | solution.py:50
where the time goes:
time: 195 us; the launch traced here: 194 us
  blocking collectives  64.7 us (33%)
  local copies, waits for them, and re-layouts  50 us (26%)
  waiting for transfers between devices  45.3 us (23%)
  starting transfers between devices  18 us (9%)
  other arithmetic  9.87 us (5%)
  loops' own time  2.81 us (1%)
  matrix products  2.52 us (1%)
    all_to_all x1, waiting for transfers between devices, shards(): lax.all_to_all(fetched, ('shard', 'sub'), split_axis=0, concat_axis=0, ti...  45.3 us
    all_gather x1, blocking collectives, combined_all(): pieces = lax.all_gather(value, axis)  33 us
    all_gather x1, blocking collectives, shards(): lax.all_gather(queries[:, :PREFIX], ('shard', 'sub'), axis=0, tiled=True)  31.7 us
    scatter x1, local copies, waits for them, and re-layouts, shards(): jnp.zeros((devices, capacity), jnp.int32).at[owners, slot_ids]  18.7 us
    gather x1, local copies, waits for them, and re-layouts, shards(): jnp.take(passages, incoming.reshape(-1), axis=0)  13.3 us
    gather x1, local copies, waits for them, and re-layouts, shards(): cand_rows = returned[owners, slot_ids].reshape(qry_dev, cands, width)  12.5 us
    all_to_all x1, starting transfers between devices, shards(): lax.all_to_all(request, ('shard', 'sub'), split_axis=0, concat_axis=0, ti...  11.1 us
    all_to_all x1, starting transfers between devices, shards(): lax.all_to_all(fetched, ('shard', 'sub'), split_axis=0, concat_axis=0, ti...  6.84 us
  transfers between devices with their start and end apart: 2, of which 1 were waited for; matrix products, arithmetic and copies ran while one was open for 3% of the time, Pallas kernels for 0%

commit v1 on v0

v1 whole, which is shorter than its diff:
```python
import jax
import jax.numpy as jnp
from jax import lax
from jax.experimental import pallas as pl
from jax.experimental.pallas import tpu as pltpu
from jax.sharding import PartitionSpec as P

NSH, NSU = 16, 8
NDEV = NSH * NSU
D = 2048
HALF = D // 2
PREFIX = 64
CANDS = 200
CAP = 8
NQ = 256
CHUNKS = 4
CW = D // CHUNKS
NEG = -3.0e38
MESH = pl.DeviceIdType.MESH
F32, BF16, I32 = jnp.float32, jnp.bfloat16, jnp.int32


def iota(shape, dim):
    return lax.broadcasted_iota(I32, shape, dim)


def dot_nt(a, b):
    return lax.dot_general(a, b, (((1,), (1,)), ((), ())), preferred_element_type=F32)


def kernel(cand_ref, q_ref, p_hbm, lse_ref, probs_ref, out_ref,
           p_v, candp, qf, qsend, code, qbuf, cbuf, q16f, q16, qall, ctile, crecv,
           st, stat1, stat1r, stat2, stat2r, codet, wt, whi, wlo,
           pool, ra, rb, zsend, zr, psend, prtile, pusend, purecv,
           p_sem, q1s, q1r, c1s, c1r, q2s, q2r, c2s, c2r, sibs, sibr,
           s1s, s1r, s2s, s2r, ps_s, ps_r, pu_s, pu_r, as_, ar_, bs_, br_, zs_, zr_):
    sh, su = lax.axis_index("shard"), lax.axis_index("sub")
    core, z = su % 2, su // 2

    def sub_peer(k):
        return (sh, su ^ k)

    def shard_peer(k):
        return (sh ^ k, su)

    barrier = pltpu.get_barrier_semaphore()

    def greet(k, c):
        pl.semaphore_signal(barrier, inc=1, device_id=shard_peer(k), device_id_type=MESH)
        return c

    def greet_sub(k, c):
        pl.semaphore_signal(barrier, inc=1, device_id=sub_peer(k), device_id_type=MESH)
        return c

    lax.fori_loop(1, NSH, greet, 0)
    lax.fori_loop(1, NSU, greet_sub, 0)
    load_p = pltpu.make_async_copy(p_hbm, p_v, p_sem)
    load_p.start()

    def loop(n, fn):
        def step(k, c):
            fn(k)
            return c
        lax.fori_loop(1, n, step, 0)

    def remote(src, dst, s, r, peer):
        return pltpu.make_async_remote_copy(src_ref=src, dst_ref=dst, send_sem=s, recv_sem=r,
                                            device_id=peer, device_id_type=MESH)

    candp[...] = jnp.full((2, 256), -1, I32)
    candp[:, :CANDS] = cand_ref[...]
    upper = jnp.where(iota((256, 256), 0) <= iota((256, 256), 1), 1.0, 0.0).astype(BF16)
    onehots, ranks = [], []
    before = jnp.zeros((128, 1), F32)
    for t in range(2):
        ids = candp[t:t + 1, :]
        dev = ids // D
        place = jnp.where(ids >= 0, (dev % NSU) * NSH + dev // NSU, -1)
        local = ids - dev * D + 1
        oh = jnp.where(iota((128, 256), 0) == place, 1.0, 0.0)
        ohb = oh.astype(BF16)
        cum = jnp.dot(ohb, upper, preferred_element_type=F32) + before
        rank = jnp.sum(oh * cum, axis=0, keepdims=True) - 1.0
        before = cum[:, 255:256]
        at = iota((CAP, 256), 0).astype(F32) == rank
        high = jnp.where(at, (local // 64).astype(F32), 0.0)
        low = jnp.where(at, (local % 64).astype(F32), 0.0)
        parts = dot_nt(jnp.concatenate([high, low], axis=0).astype(BF16), ohb)
        code[t * 8:t * 8 + 8, :] = parts[:8] * 64.0 + parts[8:]
        onehots.append(ohb)
        ranks.append(rank)

    x = q_ref[...].astype(F32)
    for r in range(8):
        qf[2 * r:2 * r + 2, :] = x[:, r * 256:(r + 1) * 256]
    qsend[...] = qf[...].astype(BF16)
    qbuf[su] = qsend[...]
    cbuf[su] = code[...]

    pl.semaphore_wait(barrier, NSH - 1 + NSU - 1)

    def d_q1(k):
        return remote(qsend, qbuf.at[su], q1s.at[k], q1r.at[k], sub_peer(k))

    def d_c1(k):
        return remote(code, cbuf.at[su], c1s.at[k], c1r.at[k], sub_peer(k))

    def start1(k):
        d_q1(k).start()
        d_c1(k).start()

    def wait1(k):
        d_q1(k).wait()
        d_c1(k).wait()

    loop(NSU, start1)
    loop(NSU, wait1)

    for i in range(NSU):
        block = qbuf[i].astype(F32)
        for r in range(8):
            for t in range(2):
                row = (i % 2) * 8 + t * 4 + i // 2
                q16f[row:row + 1, r * 256:(r + 1) * 256] = block[2 * r + t:2 * r + t + 1, :]
    for h in range(2):
        q16[h] = q16f[:, h * HALF:(h + 1) * HALF].astype(BF16)
    lane = iota((8, 128), 1)
    base = (sh % 8) * 16
    tiles = [jnp.zeros((8, 128), F32) for _ in range(NSH)]
    for i in range(NSU):
        for t in range(2):
            mine = pltpu.roll(cbuf[i, t * 8:t * 8 + 8, :], (NSU - su) * NSH, 1)
            here = lane == base + ((i % 2) * 8 + t * 4 + i // 2)
            for j in range(NSH):
                tiles[j] = jnp.where(here, jnp.broadcast_to(mine[:, j:j + 1], (8, 128)), tiles[j])
    for j in range(NSH):
        ctile[j] = tiles[j]
    qall[core, pl.ds(pl.multiple_of(sh * 16, 16), 16), :] = q16[core]
    crecv[sh] = ctile[sh]

    def d_q2(k):
        rows = pl.ds(pl.multiple_of(sh * 16, 16), 16)
        return remote(q16.at[core], qall.at[core, rows], q2s.at[k], q2r.at[k], shard_peer(k))

    def d_c2(k):
        return remote(ctile.at[sh ^ k], crecv.at[sh], c2s.at[k], c2r.at[k], shard_peer(k))

    def start2(k):
        d_q2(k).start()
        d_c2(k).start()

    def wait2(k):
        d_q2(k).wait()
        d_c2(k).wait()

    loop(NSH, start2)
    loop(NSH, wait2)
    sib = remote(qall.at[core], qall.at[core], sibs, sibr, sub_peer(1))
    sib.start()

    load_p.wait()
    ROWS = 256

    def score_half(h, add):
        def step(i, c):
            rows = pl.ds(pl.multiple_of(i * ROWS, ROWS), ROWS)
            cols = pl.ds(pl.multiple_of(h * HALF, HALF), HALF)
            part = dot_nt(p_v[rows, cols], qall[h])
            st[rows, :] = st[rows, :] + part if add else part
            return c
        lax.fori_loop(0, D // ROWS, step, 0)

    score_half(core, False)
    sib.wait()
    score_half(1 - core, True)

    first, second = crecv[0], crecv[8]
    for i in range(1, 8):
        first = first + crecv[i]
        second = second + crecv[8 + i]
    codes = jnp.concatenate([first, second], axis=1).astype(I32) - 1
    rows_of = [jnp.broadcast_to(codes[s:s + 1, :], (8, 256)) for s in range(CAP)]
    sub_iota = iota((8, 256), 0)

    def pick(i, accs):
        for j in range(4):
            start = pl.multiple_of(i * 32 + j * 8, 8)
            vals = st[pl.ds(start, 8), :]
            at = sub_iota + start
            accs = tuple(a + jnp.where(at == rows_of[s], vals, 0.0) for s, a in enumerate(accs))
        return accs

    accs = lax.fori_loop(0, D // 32, pick, tuple(jnp.zeros((8, 256), F32) for _ in range(CAP)))
    scores = jnp.concatenate([jnp.sum(a, axis=0, keepdims=True) for a in accs], axis=0) * (D ** -0.5)
    valid = codes >= 0
    masked = jnp.where(valid, scores, NEG)
    m0 = jnp.max(masked, axis=0, keepdims=True)
    l0 = jnp.sum(jnp.where(valid, jnp.exp(masked - m0), 0.0), axis=0, keepdims=True)
    stat1[0:1, :] = m0
    stat1[1:2, :] = l0
    stat1[2:8, :] = jnp.zeros((6, 256), F32)
    stat1r[su] = stat1[...]

    def d_s1(k):
        return remote(stat1, stat1r.at[su], s1s.at[k], s1r.at[k], sub_peer(k))

    loop(NSU, lambda k: d_s1(k).start())

    qp = qall[0, :, 0:128]
    qp = jnp.where(iota((NQ, 128), 1) < PREFIX, qp.astype(F32), 0.0).astype(BF16)

    def prefix(i, top):
        rows = pl.ds(pl.multiple_of(i * ROWS, ROWS), ROWS)
        part = dot_nt(p_v[rows, 0:128], qp) * (PREFIX ** -0.5)
        st[rows, :] = part
        return jnp.maximum(top, jnp.max(part.reshape(ROWS // 8, 8, 256), axis=0))

    top = lax.fori_loop(0, D // ROWS, prefix, jnp.full((8, 256), NEG, F32))
    cm = jnp.max(top, axis=0, keepdims=True)

    def expsum(i, tot):
        rows = pl.ds(pl.multiple_of(i * 64, 64), 64)
        return tot + jnp.sum(jnp.exp(st[rows, :] - cm).reshape(8, 8, 256), axis=0)

    tot = lax.fori_loop(0, D // 64, expsum, jnp.zeros((8, 256), F32))
    cl = jnp.sum(tot, axis=0, keepdims=True)

    loop(NSU, lambda k: d_s1(k).wait())

    def join(buf, n, row):
        top = buf[0, row:row + 1, :]
        for i in range(1, n):
            top = jnp.maximum(top, buf[i, row:row + 1, :])
        total = jnp.zeros((1, 256), F32)
        for i in range(n):
            total = total + buf[i, row + 1:row + 2, :] * jnp.exp(buf[i, row:row + 1, :] - top)
        return top, total

    m1, l1 = join(stat1r, NSU, 0)
    stat2[0:1, :] = m1
    stat2[1:2, :] = l1
    stat2[2:3, :] = cm
    stat2[3:4, :] = cl
    stat2[4:8, :] = jnp.zeros((4, 256), F32)
    stat2r[sh] = stat2[...]

    def d_s2(k):
        return remote(stat2, stat2r.at[sh], s2s.at[k], s2r.at[k], shard_peer(k))

    loop(NSH, lambda k: d_s2(k).start())
    codet[:, 0:8] = codes.astype(F32).T
    loop(NSH, lambda k: d_s2(k).wait())
    m2, l2 = join(stat2r, NSH, 0)
    cm2, cl2 = join(stat2r, NSH, 2)

    probs = jnp.where(valid, jnp.exp(masked - m2), 0.0) / l2
    weights = probs.astype(BF16).astype(F32)
    wt[:, 0:8] = weights.T
    psend[0] = probs[:, 0:128]
    psend[1] = probs[:, 128:256]

    def spread(i, c):
        rows = pl.ds(pl.multiple_of(i * 16, 16), 16)
        ct = codet[rows, 0:8].astype(I32)
        w = wt[rows, 0:8]
        for g in range(4):
            cols = iota((16, 512), 1) + g * 512
            val = jnp.zeros((16, 512), F32)
            for s in range(CAP):
                val = val + jnp.where(cols == ct[:, s:s + 1], w[:, s:s + 1], 0.0)
            hi = val.astype(BF16)
            whi[rows, g * 512:(g + 1) * 512] = hi
            wlo[rows, g * 512:(g + 1) * 512] = (val - hi.astype(F32)).astype(BF16)
        return c

    lax.fori_loop(0, NQ // 16, spread, 0)

    def d_a(j):
        return remote(pool.at[j, 1 - core], ra.at[j], as_.at[j], ar_.at[j], sub_peer(1))

    def d_b(j, k):
        return remote(pool.at[j, core, sh ^ k], rb.at[j, sh], bs_.at[j, k], br_.at[j, k], shard_peer(k))

    def multiply(j):
        cols = slice(j * CW, (j + 1) * CW)
        part = jnp.dot(whi[...], p_v[:, cols], preferred_element_type=F32)
        part = part + jnp.dot(wlo[...], p_v[:, cols], preferred_element_type=F32)
        for i in range(NSH):
            for c in range(2):
                pool[j, c, i] = part[i * 16 + c * 8:i * 16 + c * 8 + 8, :]
        d_a(j).start()

    def forward(j):
        d_a(j).wait()
        for i in range(NSH):
            pool[j, core, i] = pool[j, core, i] + ra[j, i]
        rb[j, sh] = pool[j, core, sh]
        loop(NSH, lambda k: d_b(j, k).start())

    def d_ps(k):
        return remote(psend.at[(sh ^ k) // 8], prtile.at[sh], ps_s.at[k], ps_r.at[k], shard_peer(k))

    multiply(0)
    for j in range(1, CHUNKS):
        multiply(j)
        forward(j - 1)
    forward(CHUNKS - 1)

    prtile[sh] = psend[sh // 8]
    loop(NSH, lambda k: d_ps(k).start())
    loop(NSH, lambda k: d_ps(k).wait())
    outs = [[jnp.zeros((8, 128), F32) for _ in range(2)] for _ in range(NSU)]
    for h in range(NSH):
        mine = pltpu.roll(prtile[h], 128 - base, 1)
        here = lane == su * NSH + h
        for d in range(NSU):
            for t in range(2):
                col = (d % 2) * 8 + t * 4 + d // 2
                outs[d][t] = jnp.where(here, jnp.broadcast_to(mine[:, col:col + 1], (8, 128)), outs[d][t])
    coarse = jnp.concatenate([cm2[:, 0:128], cm2[:, 128:256], cl2[:, 0:128], cl2[:, 128:256],
                              jnp.zeros((4, 128), F32)], axis=0)
    for d in range(NSU):
        for t in range(2):
            pusend[d, t * 8:t * 8 + 8, :] = outs[d][t]
        pusend[d, 16:24, :] = coarse
    purecv[su] = pusend[su]

    def d_pu(k):
        return remote(pusend.at[su ^ k], purecv.at[su], pu_s.at[k], pu_r.at[k], sub_peer(k))

    loop(NSU, lambda k: d_pu(k).start())

    for j in range(CHUNKS):
        loop(NSH, lambda k: d_b(j, k).wait())
        tile = rb[j, 0]
        for i in range(1, NSH):
            tile = tile + rb[j, i]
        for t in range(2):
            for i in range(4):
                zsend[i, t * 4 + j:t * 4 + j + 1, :] = tile[t * 4 + i:t * 4 + i + 1, :]
    zr[z] = zsend[z]

    def d_z(k):
        return remote(zsend.at[z ^ k], zr.at[z], zs_.at[k], zr_.at[k], sub_peer(2 * k))

    loop(4, lambda k: d_z(k).start())

    loop(NSU, lambda k: d_pu(k).wait())
    for t in range(2):
        p = purecv[0, t * 8:t * 8 + 8, :]
        for i in range(1, NSU):
            p = p + purecv[i, t * 8:t * 8 + 8, :]
        p1 = p.astype(BF16)
        rest = p - p1.astype(F32)
        p2 = rest.astype(BF16)
        p3 = (rest - p2.astype(F32)).astype(BF16)
        y = jnp.dot(jnp.concatenate([p1.astype(F32), p2.astype(F32), p3.astype(F32)], axis=0).astype(BF16),
                    onehots[t], preferred_element_type=F32)
        y = y[0:8] + y[8:16] + y[16:24]
        row = jnp.sum(jnp.where(iota((CAP, 256), 0).astype(F32) == ranks[t], y, 0.0), axis=0, keepdims=True)
        probs_ref[t:t + 1, :] = row[:, :CANDS]
    top = purecv[0, 16:18, :]
    for i in range(1, NSU):
        top = jnp.maximum(top, purecv[i, 16:18, :])
    total = jnp.zeros((2, 128), F32)
    for i in range(NSU):
        total = total + purecv[i, 18:20, :] * jnp.exp(purecv[i, 16:18, :] - top)
    lse = top + jnp.log(total)
    spot = iota((2, 128), 0) * 128 + iota((2, 128), 1)
    for t in range(2):
        mine = jnp.where(spot == sh * 16 + core * 8 + t * 4 + z, lse, 0.0)
        lse_ref[0:1, t:t + 1] = jnp.sum(mine, keepdims=True)

    loop(4, lambda k: d_z(k).wait())
    final = zr[0] + zr[1] + zr[2] + zr[3]
    for t in range(2):
        for j in range(CHUNKS):
            out_ref[t:t + 1, j * CW:(j + 1) * CW] = final[t * 4 + j:t * 4 + j + 1, :].astype(BF16)


def shards(queries, passages, candidates):
    vmem = pl.BlockSpec(memory_space=pltpu.VMEM)
    V, DMA = pltpu.VMEM, pltpu.SemaphoreType.DMA
    lse, probs, pooled = pl.pallas_call(
        kernel,
        name="retrieve",
        out_shape=(
            jax.ShapeDtypeStruct((1, 2), F32),
            jax.ShapeDtypeStruct((2, CANDS), F32),
            jax.ShapeDtypeStruct((2, D), BF16),
        ),
        in_specs=[vmem, vmem, pl.BlockSpec(memory_space=pl.ANY)],
        out_specs=(vmem, vmem, vmem),
        scratch_shapes=[
            V((D, D), BF16), V((2, 256), I32), V((16, 256), F32), V((16, 256), BF16), V((16, 128), F32),
            V((NSU, 16, 256), BF16), V((NSU, 16, 128), F32), V((16, D), F32), V((2, 16, HALF), BF16),
            V((2, NQ, HALF), BF16), V((NSH, 8, 128), F32), V((NSH, 8, 128), F32),
            V((D, NQ), F32),
            V((8, 256), F32), V((NSU, 8, 256), F32), V((8, 256), F32), V((NSH, 8, 256), F32),
            V((NQ, 128), F32), V((NQ, 128), F32), V((NQ, D), BF16), V((NQ, D), BF16),
            V((CHUNKS, 2, NSH, 8, CW), F32), V((CHUNKS, NSH, 8, CW), F32), V((CHUNKS, NSH, 8, CW), F32),
            V((4, 8, CW), F32), V((4, 8, CW), F32), V((2, 8, 128), F32), V((NSH, 8, 128), F32),
            V((NSU, 24, 128), F32), V((NSU, 24, 128), F32),
            DMA(()),
            DMA((NSU,)), DMA((NSU,)), DMA((NSU,)), DMA((NSU,)),
            DMA((NSH,)), DMA((NSH,)), DMA((NSH,)), DMA((NSH,)), DMA(()), DMA(()),
            DMA((NSU,)), DMA((NSU,)), DMA((NSH,)), DMA((NSH,)),
            DMA((NSH,)), DMA((NSH,)), DMA((NSU,)), DMA((NSU,)),
            DMA((CHUNKS,)), DMA((CHUNKS,)), DMA((CHUNKS, NSH)), DMA((CHUNKS, NSH)),
            DMA((4,)), DMA((4,)),
        ],
        compiler_params=pltpu.CompilerParams(
            collective_id=0, has_side_effects=True, vmem_limit_bytes=50 * 1024 * 1024
        ),
    )(candidates, queries, passages)
    return lse.reshape(2), probs, pooled


def solution(mesh):
    spec = P(("shard", "sub"), None)
    return jax.shard_map(shards, mesh=mesh, in_specs=(spec, spec, spec),
                         out_specs=(P(("shard", "sub")), spec, spec), check_vma=False)
```

time: 195 us -> 74.3 us (0.38)
  Pallas kernels: 0 us -> 69.6 us
  blocking collectives: 64.7 us -> 0 us
  local copies, waits for them, and re-layouts: 50 us -> 3.06 us
  waiting for transfers between devices: 45.3 us -> 0 us
  starting transfers between devices: 18 us -> 0 us
  other arithmetic: 9.87 us -> 0 us
  loops' own time: 2.81 us -> 0 us
  matrix products: 2.52 us -> 0 us
    pallas_call x0 -> x1, Pallas kernels: none -> 69.6 us  [shards(): pl.pallas_call(kernel, name='retrieve', out_shape=(jax.ShapeDtypeStruct((...]
    all_gather x2 -> x0, blocking collectives: 64.7 us -> none  [the longest x1 33 us: combined_all(): pieces = lax.all_gather(value, axis)]
    all_to_all x2 -> x0, waiting for transfers between devices: 45.3 us -> none  [the longest x1 45.3 us: shards(): lax.all_to_all(fetched, ('shard', 'sub'), split_axis=0, concat_axis=0, ti...]
    gather x2 -> x0, local copies, waits for them, and re-layouts: 25.8 us -> none  [the longest x1 13.3 us: shards(): jnp.take(passages, incoming.reshape(-1), axis=0)]
    scatter x1 -> x0, local copies, waits for them, and re-layouts: 18.7 us -> none  [shards(): jnp.zeros((devices, capacity), jnp.int32).at[owners, slot_ids]]
    all_to_all x2 -> x0, starting transfers between devices: 18 us -> none  [the longest x1 11.1 us: shards(): lax.all_to_all(request, ('shard', 'sub'), split_axis=0, concat_axis=0, ti...]
    select_n x3 -> x0, other arithmetic: 4.59 us -> none  [the longest x2 4.58 us: shards(): jnp.take(passages, incoming.reshape(-1), axis=0)]
    unnamed x7, local copies, waits for them, and re-layouts: 0.03 us -> 3.06 us
  transfers between devices with their start and end apart: 2 -> 0, of which waited for: 1 -> 0; matrix products, arithmetic and copies ran while one was open for 3% -> 0% of each run, Pallas kernels for 0% -> 0%
where the time goes in v1:
time: 74.3 us; the launch traced here: 73.3 us
  Pallas kernels  69.6 us (94%)
  local copies, waits for them, and re-layouts  3.06 us (4%)
    pallas_call x1, Pallas kernels, shards(): pl.pallas_call(kernel, name='retrieve', out_shape=(jax.ShapeDtypeStruct((...  69.6 us
    unnamed x7, local copies, waits for them, and re-layouts  3.06 us

profile of v1, /device:TPU:0, one launch (start us, length us, event | category | flops | bytes accessed | tf_op | source)
XLA Modules:
  0.0 73.3 jit_solution(6337402368765987470)
XLA Ops:
  0.6 0.0 copy-start
  0.6 0.7 copy-done
  1.3 0.0 copy-start.1
  1.3 0.7 copy-done.1
  2.0 69.6 %retrieve.1 = (f32[1,2]{1,0:T(1,128)S(1)}, f32[2,200]{1,0:T(2,128)S(1)}, bf16[2,2048]{1,0:T(2,128)(2,1)S(1)}) custom-call(s32[2,200]{1,0:T(2,128)S(1)} %copy-done.1, bf16[2,2048]{1,0:T(2,128)(2,1)S(1)} %copy-done, bf16[2048,2048]{1,0:T(8,128)(2,1)} %p_hbm.1), custom_call_target="tpu_custom_call" | custom-call | tf_op jit(solution)/shard_map/retrieve/pallas_call | solution.py:385
  71.6 0.5 copy.9
  72.1 0.6 copy.10
  72.7 0.6 copy.11
Async XLA Ops:
  0.6 0.7 copy-start
  1.3 0.7 copy-start.1

commit v2 on v1

--- a/solution.py
+++ b/solution.py
@@ -28,14 +28,17 @@
     return lax.dot_general(a, b, (((1,), (1,)), ((), ())), preferred_element_type=F32)
 
 
-def kernel(cand_ref, q_ref, p_hbm, lse_ref, probs_ref, out_ref,
-           p_v, candp, qf, qsend, code, qbuf, cbuf, q16f, q16, qall, ctile, crecv,
-           st, stat1, stat1r, stat2, stat2r, codet, wt, whi, wlo,
-           pool, ra, rb, zsend, zr, psend, prtile, pusend, purecv,
-           p_sem, q1s, q1r, c1s, c1r, q2s, q2r, c2s, c2r, sibs, sibr,
-           s1s, s1r, s2s, s2r, ps_s, ps_r, pu_s, pu_r, as_, ar_, bs_, br_, zs_, zr_):
+def kernel(cand_hbm, q_hbm, p_hbm, lse_ref, probs_ref, out_ref,
+           p_v, cand_v, q_v, candp, qf, qsend, code, qbuf, cbuf, q16f, q16, qall, ctile, crecv,
+           st, cst, stat1, stat1r, stat2, stat2r, colt, count, grown, whl,
+           pool, ra, rb, re, zsend, zr, psend, prtile, pusend, purecv,
+           p_sem, in_sem, q1s, q1r, c1s, c1r, q2s, q2r, q3s, q3r, c2s, c2r, sibs, sibr,
+           s1s, s1r, s2s, s2r, ps_s, ps_r, pu_s, pu_r, as_, ar_, bs_, br_, es_, er_, zs_, zr_):
     sh, su = lax.axis_index("shard"), lax.axis_index("sub")
     core, z = su % 2, su // 2
+    y, x = sh // 4, sh % 4
+    a1, a2 = y + core * (x - y), x + core * (y - x)
+    step1, step2 = 4 - 3 * core, 1 + 3 * core
 
     def sub_peer(k):
         return (sh, su ^ k)
@@ -43,6 +46,10 @@
     def shard_peer(k):
         return (sh ^ k, su)
 
+    load_c = pltpu.make_async_copy(cand_hbm, cand_v, in_sem.at[0])
+    load_c.start()
+    load_q = pltpu.make_async_copy(q_hbm, q_v, in_sem.at[1])
+    load_q.start()
     barrier = pltpu.get_barrier_semaphore()
 
     def greet(k, c):
@@ -69,7 +76,8 @@
                                             device_id=peer, device_id_type=MESH)
 
     candp[...] = jnp.full((2, 256), -1, I32)
-    candp[:, :CANDS] = cand_ref[...]
+    load_c.wait()
+    candp[:, :CANDS] = cand_v[...]
     upper = jnp.where(iota((256, 256), 0) <= iota((256, 256), 1), 1.0, 0.0).astype(BF16)
     onehots, ranks = [], []
     before = jnp.zeros((128, 1), F32)
@@ -91,9 +99,10 @@
         onehots.append(ohb)
         ranks.append(rank)
 
-    x = q_ref[...].astype(F32)
+    load_q.wait()
+    qs = q_v[...].astype(F32)
     for r in range(8):
-        qf[2 * r:2 * r + 2, :] = x[:, r * 256:(r + 1) * 256]
+        qf[2 * r:2 * r + 2, :] = qs[:, r * 256:(r + 1) * 256]
     qsend[...] = qf[...].astype(BF16)
     qbuf[su] = qsend[...]
     cbuf[su] = code[...]
@@ -139,28 +148,32 @@
     qall[core, pl.ds(pl.multiple_of(sh * 16, 16), 16), :] = q16[core]
     crecv[sh] = ctile[sh]
 
+    def q_block(j):
+        return qall.at[core, pl.ds(pl.multiple_of((sh ^ (j * step1)) * 16, 16), 16)]
+
     def d_q2(k):
-        rows = pl.ds(pl.multiple_of(sh * 16, 16), 16)
-        return remote(q16.at[core], qall.at[core, rows], q2s.at[k], q2r.at[k], shard_peer(k))
+        return remote(q_block(0), q_block(0), q2s.at[k], q2r.at[k], shard_peer(k * step1))
+
+    def d_q3(j, k):
+        return remote(q_block(j), q_block(j), q3s.at[j, k], q3r.at[j, k], shard_peer(k * step2))
 
     def d_c2(k):
         return remote(ctile.at[sh ^ k], crecv.at[sh], c2s.at[k], c2r.at[k], shard_peer(k))
 
-    def start2(k):
-        d_q2(k).start()
-        d_c2(k).start()
-
-    def wait2(k):
-        d_q2(k).wait()
-        d_c2(k).wait()
-
-    loop(NSH, start2)
-    loop(NSH, wait2)
+    loop(4, lambda k: d_q2(k).start())
+    loop(4, lambda k: d_q3(0, k).start())
+    loop(NSH, lambda k: d_c2(k).start())
+    for j in range(1, 4):
+        d_q2(j).wait()
+        loop(4, lambda k: d_q3(j, k).start())
+    for j in range(4):
+        loop(4, lambda k: d_q3(j, k).wait())
+    loop(NSH, lambda k: d_c2(k).wait())
     sib = remote(qall.at[core], qall.at[core], sibs, sibr, sub_peer(1))
     sib.start()
 
     load_p.wait()
-    ROWS = 256
+    ROWS = 512
 
     def score_half(h, add):
         def step(i, c):
@@ -213,7 +226,7 @@
     def prefix(i, top):
         rows = pl.ds(pl.multiple_of(i * ROWS, ROWS), ROWS)
         part = dot_nt(p_v[rows, 0:128], qp) * (PREFIX ** -0.5)
-        st[rows, :] = part
+        cst[rows, :] = part
         return jnp.maximum(top, jnp.max(part.reshape(ROWS // 8, 8, 256), axis=0))
 
     top = lax.fori_loop(0, D // ROWS, prefix, jnp.full((8, 256), NEG, F32))
@@ -221,7 +234,7 @@
 
     def expsum(i, tot):
         rows = pl.ds(pl.multiple_of(i * 64, 64), 64)
-        return tot + jnp.sum(jnp.exp(st[rows, :] - cm).reshape(8, 8, 256), axis=0)
+        return tot + jnp.sum(jnp.exp(cst[rows, :] - cm).reshape(8, 8, 256), axis=0)
 
     tot = lax.fori_loop(0, D // 64, expsum, jnp.zeros((8, 256), F32))
     cl = jnp.sum(tot, axis=0, keepdims=True)
@@ -249,29 +262,57 @@
         return remote(stat2, stat2r.at[sh], s2s.at[k], s2r.at[k], shard_peer(k))
 
     loop(NSH, lambda k: d_s2(k).start())
-    codet[:, 0:8] = codes.astype(F32).T
+
+    colt[:, 0:8] = codes.astype(F32).T
+    colt[:, 8:16] = jnp.broadcast_to(m0, (8, 256)).T
+
+    def flip(i, c):
+        rows = pl.ds(pl.multiple_of(i * 256, 256), 256)
+        grown[:, rows] = st[rows, :].T
+        return c
+
+    lax.fori_loop(0, D // 256, flip, 0)
+
+    def tally(i, c):
+        rows = pl.ds(pl.multiple_of(i * 16, 16), 16)
+        ct = colt[rows, 0:8].astype(I32)
+        top = colt[rows, 8:9]
+        for g in range(4):
+            cols = iota((16, 512), 1) + g * 512
+            here = slice(g * 512, (g + 1) * 512)
+            val = jnp.zeros((16, 512), F32)
+            for s in range(CAP):
+                val = val + jnp.where(cols == ct[:, s:s + 1], 1.0, 0.0)
+            count[rows, here] = val
+            grown[rows, here] = jnp.where(val > 0.0, jnp.exp(grown[rows, here] * (D ** -0.5) - top), 0.0)
+        return c
+
+    lax.fori_loop(0, NQ // 16, tally, 0)
     loop(NSH, lambda k: d_s2(k).wait())
     m2, l2 = join(stat2r, NSH, 0)
     cm2, cl2 = join(stat2r, NSH, 2)
 
-    probs = jnp.where(valid, jnp.exp(masked - m2), 0.0) / l2
-    weights = probs.astype(BF16).astype(F32)
-    wt[:, 0:8] = weights.T
+    scale = jnp.exp(m0 - m2) / l2
+    probs = jnp.where(valid, jnp.exp(masked - m0), 0.0) * scale
     psend[0] = probs[:, 0:128]
     psend[1] = probs[:, 128:256]
+    prtile[sh] = psend[sh // 8]
+
+    def d_ps(k):
+        return remote(psend.at[(sh ^ k) // 8], prtile.at[sh], ps_s.at[k], ps_r.at[k], shard_peer(k))
+
+    loop(NSH, lambda k: d_ps(k).start())
+
+    colt[:, 16:24] = jnp.broadcast_to(scale, (8, 256)).T
 
     def spread(i, c):
         rows = pl.ds(pl.multiple_of(i * 16, 16), 16)
-        ct = codet[rows, 0:8].astype(I32)
-        w = wt[rows, 0:8]
-        for g in range(4):
-            cols = iota((16, 512), 1) + g * 512
-            val = jnp.zeros((16, 512), F32)
-            for s in range(CAP):
-                val = val + jnp.where(cols == ct[:, s:s + 1], w[:, s:s + 1], 0.0)
-            hi = val.astype(BF16)
-            whi[rows, g * 512:(g + 1) * 512] = hi
-            wlo[rows, g * 512:(g + 1) * 512] = (val - hi.astype(F32)).astype(BF16)
+        lows = pl.ds(pl.multiple_of(NQ + i * 16, 16), 16)
+        f = colt[rows, 16:17]
+        val = (grown[rows, :] * f).astype(BF16).astype(F32) * count[rows, :]
+        hi = val.astype(BF16)
+        whl[rows, :] = hi
+        whl[lows, :] = (val - hi.astype(F32)).astype(BF16)
         return c
 
     lax.fori_loop(0, NQ // 16, spread, 0)
@@ -280,35 +321,50 @@
         return remote(pool.at[j, 1 - core], ra.at[j], as_.at[j], ar_.at[j], sub_peer(1))
 
     def d_b(j, k):
-        return remote(pool.at[j, core, sh ^ k], rb.at[j, sh], bs_.at[j, k], br_.at[j, k], shard_peer(k))
+        return remote(pool.at[j, core, pl.ds((a1 ^ k) * 4, 4)], rb.at[j, pl.ds(k * 4, 4)],
+                      bs_.at[j, k], br_.at[j, k], shard_peer(k * step1))
+
+    def d_e(j, k):
+        return remote(rb.at[j, a2 ^ k], re.at[j, k], es_.at[j, k], er_.at[j, k], shard_peer(k * step2))
 
     def multiply(j):
         cols = slice(j * CW, (j + 1) * CW)
-        part = jnp.dot(whi[...], p_v[:, cols], preferred_element_type=F32)
-        part = part + jnp.dot(wlo[...], p_v[:, cols], preferred_element_type=F32)
+        part = jnp.dot(whl[...], p_v[:, cols], preferred_element_type=F32)
+        part = part[:NQ] + part[NQ:]
         for i in range(NSH):
             for c in range(2):
-                pool[j, c, i] = part[i * 16 + c * 8:i * 16 + c * 8 + 8, :]
+                pool[j, c, i if c == 0 else (i % 4) * 4 + i // 4] = part[i * 16 + c * 8:i * 16 + c * 8 + 8, :]
         d_a(j).start()
 
     def forward(j):
         d_a(j).wait()
         for i in range(NSH):
             pool[j, core, i] = pool[j, core, i] + ra[j, i]
-        rb[j, sh] = pool[j, core, sh]
-        loop(NSH, lambda k: d_b(j, k).start())
-
-    def d_ps(k):
-        return remote(psend.at[(sh ^ k) // 8], prtile.at[sh], ps_s.at[k], ps_r.at[k], shard_peer(k))
+        loop(4, lambda k: d_b(j, k).start())
+
+    def second(j):
+        loop(4, lambda k: d_b(j, k).wait())
+        for i in range(4):
+            rb[j, i] = pool[j, core, a1 * 4 + i] + rb[j, 4 + i] + rb[j, 8 + i] + rb[j, 12 + i]
+        loop(4, lambda k: d_e(j, k).start())
+
+    def third(j):
+        loop(4, lambda k: d_e(j, k).wait())
+        tile = rb[j, a2] + re[j, 1] + re[j, 2] + re[j, 3]
+        for t in range(2):
+            for i in range(4):
+                zsend[i, t * 4 + j:t * 4 + j + 1, :] = tile[t * 4 + i:t * 4 + i + 1, :]
 
     multiply(0)
-    for j in range(1, CHUNKS):
-        multiply(j)
-        forward(j - 1)
-    forward(CHUNKS - 1)
-
-    prtile[sh] = psend[sh // 8]
-    loop(NSH, lambda k: d_ps(k).start())
+    multiply(1)
+    forward(0)
+    multiply(2)
+    forward(1)
+    multiply(3)
+    forward(2)
+    second(0)
+    forward(3)
+
     loop(NSH, lambda k: d_ps(k).wait())
     outs = [[jnp.zeros((8, 128), F32) for _ in range(2)] for _ in range(NSU)]
     for h in range(NSH):
@@ -331,14 +387,13 @@
 
     loop(NSU, lambda k: d_pu(k).start())
 
-    for j in range(CHUNKS):
-        loop(NSH, lambda k: d_b(j, k).wait())
-        tile = rb[j, 0]
-        for i in range(1, NSH):
-            tile = tile + rb[j, i]
-        for t in range(2):
-            for i in range(4):
-                zsend[i, t * 4 + j:t * 4 + j + 1, :] = tile[t * 4 + i:t * 4 + i + 1, :]
+    second(1)
+    third(0)
+    second(2)
+    third(1)
+    second(3)
+    third(2)
+    third(3)
     zr[z] = zsend[z]
 
     def d_z(k):
@@ -390,24 +445,25 @@
             jax.ShapeDtypeStruct((2, CANDS), F32),
             jax.ShapeDtypeStruct((2, D), BF16),
         ),
-        in_specs=[vmem, vmem, pl.BlockSpec(memory_space=pl.ANY)],
+        in_specs=[pl.BlockSpec(memory_space=pl.ANY)] * 3,
         out_specs=(vmem, vmem, vmem),
         scratch_shapes=[
-            V((D, D), BF16), V((2, 256), I32), V((16, 256), F32), V((16, 256), BF16), V((16, 128), F32),
+            V((D, D), BF16), V((2, CANDS), I32), V((2, D), BF16), V((2, 256), I32), V((16, 256), F32), V((16, 256), BF16), V((16, 128), F32),
             V((NSU, 16, 256), BF16), V((NSU, 16, 128), F32), V((16, D), F32), V((2, 16, HALF), BF16),
             V((2, NQ, HALF), BF16), V((NSH, 8, 128), F32), V((NSH, 8, 128), F32),
-            V((D, NQ), F32),
+            V((D, NQ), F32), V((D, NQ), F32),
             V((8, 256), F32), V((NSU, 8, 256), F32), V((8, 256), F32), V((NSH, 8, 256), F32),
-            V((NQ, 128), F32), V((NQ, 128), F32), V((NQ, D), BF16), V((NQ, D), BF16),
+            V((NQ, 128), F32), V((NQ, D), F32), V((NQ, D), F32), V((2 * NQ, D), BF16),
             V((CHUNKS, 2, NSH, 8, CW), F32), V((CHUNKS, NSH, 8, CW), F32), V((CHUNKS, NSH, 8, CW), F32),
+            V((CHUNKS, 4, 8, CW), F32),
             V((4, 8, CW), F32), V((4, 8, CW), F32), V((2, 8, 128), F32), V((NSH, 8, 128), F32),
             V((NSU, 24, 128), F32), V((NSU, 24, 128), F32),
-            DMA(()),
+            DMA(()), DMA((2,)),
             DMA((NSU,)), DMA((NSU,)), DMA((NSU,)), DMA((NSU,)),
-            DMA((NSH,)), DMA((NSH,)), DMA((NSH,)), DMA((NSH,)), DMA(()), DMA(()),
+            DMA((4,)), DMA((4,)), DMA((4, 4)), DMA((4, 4)), DMA((NSH,)), DMA((NSH,)), DMA(()), DMA(()),
             DMA((NSU,)), DMA((NSU,)), DMA((NSH,)), DMA((NSH,)),
             DMA((NSH,)), DMA((NSH,)), DMA((NSU,)), DMA((NSU,)),
-            DMA((CHUNKS,)), DMA((CHUNKS,)), DMA((CHUNKS, NSH)), DMA((CHUNKS, NSH)),
+            DMA((CHUNKS,)), DMA((CHUNKS,)), DMA((CHUNKS, 4)), DMA((CHUNKS, 4)), DMA((CHUNKS, 4)), DMA((CHUNKS, 4)),
             DMA((4,)), DMA((4,)),
         ],
         compiler_params=pltpu.CompilerParams(

time: 74.3 us -> 64.9 us (0.87); the launches traced: 73.3 us -> 64.7 us
  Pallas kernels: 69.6 us -> 61 us
    pallas_call x1, Pallas kernels: 69.6 us -> 61 us  [shards(): pl.pallas_call(kernel, name='retrieve', out_shape=(jax.ShapeDtypeStruct((...]
where the time goes in v2:
time: 64.9 us; the launch traced here: 64.7 us
  Pallas kernels  61 us (94%)
  local copies, waits for them, and re-layouts  3.06 us (5%)
  between operations  0.65 us (1%)
    pallas_call x1, Pallas kernels, shards(): pl.pallas_call(kernel, name='retrieve', out_shape=(jax.ShapeDtypeStruct((...  61 us
    unnamed x7, local copies, waits for them, and re-layouts  3.06 us

profile of v2, /device:TPU:0, one launch (start us, length us, event | category | flops | bytes accessed | tf_op | source)
XLA Modules:
  0.0 64.7 jit_solution(5809955321146822874)
XLA Ops:
  0.6 0.0 copy-start
  0.6 0.7 %copy-done = bf16[2,2048]{1,0:T(2,128)(2,1)S(1)} copy-done((bf16[2,2048]{1,0:T(2,128)(2,1)S(1)}, bf16[2,2048]{1,0:T(2,128)(2,1)}, u32[]{:S(2)}) %copy-start) | copy-done | bytes 8216
  1.3 0.0 copy-start.1
  1.3 0.7 %copy-done.1 = s32[2,200]{1,0:T(2,128)S(1)} copy-done((s32[2,200]{1,0:T(2,128)S(1)}, s32[2,200]{1,0:T(2,128)}, u32[]{:S(2)}) %copy-start.1) | copy-done | bytes 1624
  2.0 61.0 %retrieve.1 = (f32[1,2]{1,0:T(1,128)S(1)}, f32[2,200]{1,0:T(2,128)S(1)}, bf16[2,2048]{1,0:T(2,128)(2,1)S(1)}) custom-call(s32[2,200]{1,0:T(2,128)S(1)} %copy-done.1, bf16[2,2048]{1,0:T(2,128)(2,1)S(1)} %copy-done, bf16[2048,2048]{1,0:T(8,128)(2,1)} %p_hbm.1), custom_call_target="tpu_custom_call" | custom-call | tf_op jit(solution)/shard_map/retrieve/pallas_call | solution.py:440
  63.0 0.5 copy.9
  63.6 0.6 copy.10
  64.1 0.6 copy.11
Async XLA Ops:
  0.6 0.7 %copy-start = (bf16[2,2048]{1,0:T(2,128)(2,1)S(1)}, bf16[2,2048]{1,0:T(2,128)(2,1)}, u32[]{:S(2)}) copy-start(bf16[2,2048]{1,0:T(2,128)(2,1)} %q_hbm.1) | copy-start | bytes 24580
  1.3 0.7 %copy-start.1 = (s32[2,200]{1,0:T(2,128)S(1)}, s32[2,200]{1,0:T(2,128)}, u32[]{:S(2)}) copy-start(s32[2,200]{1,0:T(2,128)} %cand_hbm.1) | copy-start | bytes 4804

commit v3 on v2

--- a/solution.py
+++ b/solution.py
@@ -8,13 +8,15 @@
 NSH, NSU = 16, 8
 NDEV = NSH * NSU
 D = 2048
-HALF = D // 2
+QW = D // 4
+LAST = 256
 PREFIX = 64
 CANDS = 200
 CAP = 8
 NQ = 256
 CHUNKS = 4
 CW = D // CHUNKS
+TWO_HOP = CHUNKS - 1
 NEG = -3.0e38
 MESH = pl.DeviceIdType.MESH
 F32, BF16, I32 = jnp.float32, jnp.bfloat16, jnp.int32
@@ -31,9 +33,9 @@
 def kernel(cand_hbm, q_hbm, p_hbm, lse_ref, probs_ref, out_ref,
            p_v, cand_v, q_v, candp, qf, qsend, code, qbuf, cbuf, q16f, q16, qall, ctile, crecv,
            st, cst, stat1, stat1r, stat2, stat2r, colt, count, grown, whl,
-           pool, ra, rb, re, zsend, zr, psend, prtile, pusend, purecv,
+           pool, ra, rb, re, zsend, zr, lsend, lrecv, psend, prtile, pusend, purecv,
            p_sem, in_sem, q1s, q1r, c1s, c1r, q2s, q2r, q3s, q3r, c2s, c2r, sibs, sibr,
-           s1s, s1r, s2s, s2r, ps_s, ps_r, pu_s, pu_r, as_, ar_, bs_, br_, es_, er_, zs_, zr_):
+           s1s, s1r, s2s, s2r, ps_s, ps_r, pu_s, pu_r, as_, ar_, bs_, br_, es_, er_, zs_, zr_, ls_, lr_):
     sh, su = lax.axis_index("shard"), lax.axis_index("sub")
     core, z = su % 2, su // 2
     y, x = sh // 4, sh % 4
@@ -46,10 +48,6 @@
     def shard_peer(k):
         return (sh ^ k, su)
 
-    load_c = pltpu.make_async_copy(cand_hbm, cand_v, in_sem.at[0])
-    load_c.start()
-    load_q = pltpu.make_async_copy(q_hbm, q_v, in_sem.at[1])
-    load_q.start()
     barrier = pltpu.get_barrier_semaphore()
 
     def greet(k, c):
@@ -66,18 +64,31 @@
     load_p.start()
 
     def loop(n, fn):
-        def step(k, c):
+        for k in range(1, n):
             fn(k)
-            return c
-        lax.fori_loop(1, n, step, 0)
 
     def remote(src, dst, s, r, peer):
         return pltpu.make_async_remote_copy(src_ref=src, dst_ref=dst, send_sem=s, recv_sem=r,
                                             device_id=peer, device_id_type=MESH)
 
+    qs = q_hbm[...].astype(F32)
+    for r in range(8):
+        qf[2 * r:2 * r + 2, :] = qs[:, r * 256:(r + 1) * 256]
+    qsend[...] = qf[...].astype(BF16)
+    qbuf[su] = qsend[...]
+
+    pl.semaphore_wait(barrier, NSH - 1 + NSU - 1)
+
+    def d_q1(k):
+        return remote(qsend, qbuf.at[su], q1s.at[k], q1r.at[k], sub_peer(k))
+
+    def d_c1(k):
+        return remote(code, cbuf.at[su], c1s.at[k], c1r.at[k], sub_peer(k))
+
+    loop(NSU, lambda k: d_q1(k).start())
+
     candp[...] = jnp.full((2, 256), -1, I32)
-    load_c.wait()
-    candp[:, :CANDS] = cand_v[...]
+    candp[:, :CANDS] = cand_hbm[...]
     upper = jnp.where(iota((256, 256), 0) <= iota((256, 256), 1), 1.0, 0.0).astype(BF16)
     onehots, ranks = [], []
     before = jnp.zeros((128, 1), F32)
@@ -99,41 +110,39 @@
         onehots.append(ohb)
         ranks.append(rank)
 
-    load_q.wait()
-    qs = q_v[...].astype(F32)
-    for r in range(8):
-        qf[2 * r:2 * r + 2, :] = qs[:, r * 256:(r + 1) * 256]
-    qsend[...] = qf[...].astype(BF16)
-    qbuf[su] = qsend[...]
     cbuf[su] = code[...]
-
-    pl.semaphore_wait(barrier, NSH - 1 + NSU - 1)
-
-    def d_q1(k):
-        return remote(qsend, qbuf.at[su], q1s.at[k], q1r.at[k], sub_peer(k))
-
-    def d_c1(k):
-        return remote(code, cbuf.at[su], c1s.at[k], c1r.at[k], sub_peer(k))
-
-    def start1(k):
-        d_q1(k).start()
-        d_c1(k).start()
-
-    def wait1(k):
-        d_q1(k).wait()
-        d_c1(k).wait()
-
-    loop(NSU, start1)
-    loop(NSU, wait1)
-
+    loop(NSU, lambda k: d_c1(k).start())
+    loop(NSU, lambda k: d_q1(k).wait())
     for i in range(NSU):
         block = qbuf[i].astype(F32)
         for r in range(8):
             for t in range(2):
                 row = (i % 2) * 8 + t * 4 + i // 2
                 q16f[row:row + 1, r * 256:(r + 1) * 256] = block[2 * r + t:2 * r + t + 1, :]
-    for h in range(2):
-        q16[h] = q16f[:, h * HALF:(h + 1) * HALF].astype(BF16)
+    for h in range(4):
+        q16[h] = q16f[:, h * QW:(h + 1) * QW].astype(BF16)
+    for c in range(2):
+        qall[core * 2 + c, pl.ds(pl.multiple_of(sh * 16, 16), 16), :] = q16[core * 2 + c]
+
+    def q_block(j):
+        return qall.at[pl.ds(core * 2, 2), pl.ds(pl.multiple_of((sh ^ (j * step1)) * 16, 16), 16)]
+
+    def d_q2(k):
+        return remote(q_block(0), q_block(0), q2s.at[k], q2r.at[k], shard_peer(k * step1))
+
+    def d_q3(j, k):
+        return remote(q_block(j), q_block(j), q3s.at[j, k], q3r.at[j, k], shard_peer(k * step2))
+
+    def d_c2(k):
+        return remote(ctile.at[sh ^ k], crecv.at[sh], c2s.at[k], c2r.at[k], shard_peer(k))
+
+    loop(4, lambda k: d_q2(k).start())
+    loop(4, lambda k: d_q3(0, k).start())
+    for j in range(1, 4):
+        d_q2(j).wait()
+        loop(4, lambda k: d_q3(j, k).start())
+
+    loop(NSU, lambda k: d_c1(k).wait())
     lane = iota((8, 128), 1)
     base = (sh % 8) * 16
     tiles = [jnp.zeros((8, 128), F32) for _ in range(NSH)]
@@ -145,68 +154,59 @@
                 tiles[j] = jnp.where(here, jnp.broadcast_to(mine[:, j:j + 1], (8, 128)), tiles[j])
     for j in range(NSH):
         ctile[j] = tiles[j]
-    qall[core, pl.ds(pl.multiple_of(sh * 16, 16), 16), :] = q16[core]
     crecv[sh] = ctile[sh]
-
-    def q_block(j):
-        return qall.at[core, pl.ds(pl.multiple_of((sh ^ (j * step1)) * 16, 16), 16)]
-
-    def d_q2(k):
-        return remote(q_block(0), q_block(0), q2s.at[k], q2r.at[k], shard_peer(k * step1))
-
-    def d_q3(j, k):
-        return remote(q_block(j), q_block(j), q3s.at[j, k], q3r.at[j, k], shard_peer(k * step2))
-
-    def d_c2(k):
-        return remote(ctile.at[sh ^ k], crecv.at[sh], c2s.at[k], c2r.at[k], shard_peer(k))
-
-    loop(4, lambda k: d_q2(k).start())
-    loop(4, lambda k: d_q3(0, k).start())
     loop(NSH, lambda k: d_c2(k).start())
-    for j in range(1, 4):
-        d_q2(j).wait()
-        loop(4, lambda k: d_q3(j, k).start())
     for j in range(4):
         loop(4, lambda k: d_q3(j, k).wait())
+    def d_sib(c):
+        part = qall.at[core * 2 + c]
+        return remote(part, part, sibs.at[c], sibr.at[c], sub_peer(1))
+
+    d_sib(0).start()
+    d_sib(1).start()
+    load_p.wait()
+
+    def score(h, rows):
+        cols = pl.ds(pl.multiple_of(h * QW, QW), QW)
+        return dot_nt(p_v[rows, cols], qall[h])
+
+    def score_half(i, c):
+        rows = pl.ds(pl.multiple_of(i * 512, 512), 512)
+        st[rows, :] = score(core * 2, rows) + score(core * 2 + 1, rows)
+        return c
+
+    def score_third(i, c):
+        rows = pl.ds(pl.multiple_of(i * 512, 512), 512)
+        st[rows, :] = st[rows, :] + score((1 - core) * 2, rows)
+        return c
+
+    lax.fori_loop(0, D // 512, score_half, 0)
     loop(NSH, lambda k: d_c2(k).wait())
-    sib = remote(qall.at[core], qall.at[core], sibs, sibr, sub_peer(1))
-    sib.start()
-
-    load_p.wait()
-    ROWS = 512
-
-    def score_half(h, add):
-        def step(i, c):
-            rows = pl.ds(pl.multiple_of(i * ROWS, ROWS), ROWS)
-            cols = pl.ds(pl.multiple_of(h * HALF, HALF), HALF)
-            part = dot_nt(p_v[rows, cols], qall[h])
-            st[rows, :] = st[rows, :] + part if add else part
-            return c
-        lax.fori_loop(0, D // ROWS, step, 0)
-
-    score_half(core, False)
-    sib.wait()
-    score_half(1 - core, True)
-
-    first, second = crecv[0], crecv[8]
+    first, second_ = crecv[0], crecv[8]
     for i in range(1, 8):
         first = first + crecv[i]
-        second = second + crecv[8 + i]
-    codes = jnp.concatenate([first, second], axis=1).astype(I32) - 1
+        second_ = second_ + crecv[8 + i]
+    codes = jnp.concatenate([first, second_], axis=1).astype(I32) - 1
+    valid = codes >= 0
     rows_of = [jnp.broadcast_to(codes[s:s + 1, :], (8, 256)) for s in range(CAP)]
     sub_iota = iota((8, 256), 0)
-
-    def pick(i, accs):
-        for j in range(4):
-            start = pl.multiple_of(i * 32 + j * 8, 8)
-            vals = st[pl.ds(start, 8), :]
-            at = sub_iota + start
-            accs = tuple(a + jnp.where(at == rows_of[s], vals, 0.0) for s, a in enumerate(accs))
+    d_sib(0).wait()
+    lax.fori_loop(0, D // 512, score_third, 0)
+    d_sib(1).wait()
+
+    def score_last(i, accs):
+        base_row = pl.multiple_of(i * LAST, LAST)
+        rows = pl.ds(base_row, LAST)
+        vals = st[rows, :] + score((1 - core) * 2 + 1, rows)
+        st[rows, :] = vals
+        for j in range(LAST // 8):
+            at = sub_iota + (base_row + j * 8)
+            part = vals[j * 8:j * 8 + 8, :]
+            accs = tuple(jnp.where(at == rows_of[s], part, a) for s, a in enumerate(accs))
         return accs
 
-    accs = lax.fori_loop(0, D // 32, pick, tuple(jnp.zeros((8, 256), F32) for _ in range(CAP)))
+    accs = lax.fori_loop(0, D // LAST, score_last, tuple(jnp.zeros((8, 256), F32) for _ in range(CAP)))
     scores = jnp.concatenate([jnp.sum(a, axis=0, keepdims=True) for a in accs], axis=0) * (D ** -0.5)
-    valid = codes >= 0
     masked = jnp.where(valid, scores, NEG)
     m0 = jnp.max(masked, axis=0, keepdims=True)
     l0 = jnp.sum(jnp.where(valid, jnp.exp(masked - m0), 0.0), axis=0, keepdims=True)
@@ -224,12 +224,12 @@
     qp = jnp.where(iota((NQ, 128), 1) < PREFIX, qp.astype(F32), 0.0).astype(BF16)
 
     def prefix(i, top):
-        rows = pl.ds(pl.multiple_of(i * ROWS, ROWS), ROWS)
+        rows = pl.ds(pl.multiple_of(i * 512, 512), 512)
         part = dot_nt(p_v[rows, 0:128], qp) * (PREFIX ** -0.5)
         cst[rows, :] = part
-        return jnp.maximum(top, jnp.max(part.reshape(ROWS // 8, 8, 256), axis=0))
-
-    top = lax.fori_loop(0, D // ROWS, prefix, jnp.full((8, 256), NEG, F32))
+        return jnp.maximum(top, jnp.max(part.reshape(64, 8, 256), axis=0))
+
+    top = lax.fori_loop(0, D // 512, prefix, jnp.full((8, 256), NEG, F32))
     cm = jnp.max(top, axis=0, keepdims=True)
 
     def expsum(i, tot):
@@ -265,6 +265,10 @@
 
     colt[:, 0:8] = codes.astype(F32).T
     colt[:, 8:16] = jnp.broadcast_to(m0, (8, 256)).T
+    times = jnp.zeros((CAP, 256), F32)
+    for s in range(CAP):
+        times = times + jnp.where(codes == rows_of[s], 1.0, 0.0)
+    colt[:, 16:24] = times.T
 
     def flip(i, c):
         rows = pl.ds(pl.multiple_of(i * 256, 256), 256)
@@ -277,12 +281,13 @@
         rows = pl.ds(pl.multiple_of(i * 16, 16), 16)
         ct = colt[rows, 0:8].astype(I32)
         top = colt[rows, 8:9]
+        ti = colt[rows, 16:24]
         for g in range(4):
             cols = iota((16, 512), 1) + g * 512
             here = slice(g * 512, (g + 1) * 512)
             val = jnp.zeros((16, 512), F32)
             for s in range(CAP):
-                val = val + jnp.where(cols == ct[:, s:s + 1], 1.0, 0.0)
+                val = jnp.where(cols == ct[:, s:s + 1], ti[:, s:s + 1], val)
             count[rows, here] = val
             grown[rows, here] = jnp.where(val > 0.0, jnp.exp(grown[rows, here] * (D ** -0.5) - top), 0.0)
         return c
@@ -353,7 +358,21 @@
         tile = rb[j, a2] + re[j, 1] + re[j, 2] + re[j, 3]
         for t in range(2):
             for i in range(4):
-                zsend[i, t * 4 + j:t * 4 + j + 1, :] = tile[t * 4 + i:t * 4 + i + 1, :]
+                zsend[i, t * 8 + j:t * 8 + j + 1, :] = tile[t * 4 + i:t * 4 + i + 1, :]
+
+    def at_once(j):
+        loop(4, lambda k: d_b(j, k).wait())
+        for i in range(4):
+            tile = pool[j, core, a1 * 4 + i] + rb[j, 4 + i] + rb[j, 8 + i] + rb[j, 12 + i]
+            for t in range(2):
+                for e in range(4):
+                    for g in range(CW // 128):
+                        row = ((j - TWO_HOP) * 2 + t) * (CW // 128) + g
+                        lsend[i * 4 + e, row:row + 1, :] = tile[t * 4 + e:t * 4 + e + 1, g * 128:(g + 1) * 128]
+
+    def d_l(k):
+        return remote(lsend.at[(a2 ^ (k // 4)) * 4 + (z ^ (k % 4))], lrecv.at[a2 * 4 + z], ls_.at[k], lr_.at[k],
+                      (sh ^ ((k // 4) * step2), su ^ (2 * (k % 4))))
 
     multiply(0)
     multiply(1)
@@ -364,6 +383,7 @@
     forward(2)
     second(0)
     forward(3)
+    second(1)
 
     loop(NSH, lambda k: d_ps(k).wait())
     outs = [[jnp.zeros((8, 128), F32) for _ in range(2)] for _ in range(NSU)]
@@ -387,13 +407,16 @@
 
     loop(NSU, lambda k: d_pu(k).start())
 
-    second(1)
+    second(2)
     third(0)
-    second(2)
     third(1)
-    second(3)
+    at_once(3)
+    lrecv[a2 * 4 + z] = lsend[a2 * 4 + z]
+    loop(NSH, lambda k: d_l(k).start())
     third(2)
-    third(3)
+    for i in range(4):
+        zsend[i, TWO_HOP:8, :] = jnp.zeros((8 - TWO_HOP, CW), F32)
+        zsend[i, 8 + TWO_HOP:16, :] = jnp.zeros((8 - TWO_HOP, CW), F32)
     zr[z] = zsend[z]
 
     def d_z(k):
@@ -430,8 +453,17 @@
     loop(4, lambda k: d_z(k).wait())
     final = zr[0] + zr[1] + zr[2] + zr[3]
     for t in range(2):
-        for j in range(CHUNKS):
-            out_ref[t:t + 1, j * CW:(j + 1) * CW] = final[t * 4 + j:t * 4 + j + 1, :].astype(BF16)
+        for j in range(TWO_HOP):
+            out_ref[t:t + 1, j * CW:(j + 1) * CW] = final[t * 8 + j:t * 8 + j + 1, :].astype(BF16)
+    loop(NSH, lambda k: d_l(k).wait())
+    final = lrecv[0]
+    for i in range(1, NSH):
+        final = final + lrecv[i]
+    for j in range(TWO_HOP, CHUNKS):
+        for t in range(2):
+            for g in range(CW // 128):
+                row = ((j - TWO_HOP) * 2 + t) * (CW // 128) + g
+                out_ref[t:t + 1, j * CW + g * 128:j * CW + (g + 1) * 128] = final[row:row + 1, :].astype(BF16)
 
 
 def shards(queries, passages, candidates):
@@ -445,26 +477,26 @@
             jax.ShapeDtypeStruct((2, CANDS), F32),
             jax.ShapeDtypeStruct((2, D), BF16),
         ),
-        in_specs=[pl.BlockSpec(memory_space=pl.ANY)] * 3,
+        in_specs=[vmem, vmem, pl.BlockSpec(memory_space=pl.ANY)],
         out_specs=(vmem, vmem, vmem),
         scratch_shapes=[
             V((D, D), BF16), V((2, CANDS), I32), V((2, D), BF16), V((2, 256), I32), V((16, 256), F32), V((16, 256), BF16), V((16, 128), F32),
-            V((NSU, 16, 256), BF16), V((NSU, 16, 128), F32), V((16, D), F32), V((2, 16, HALF), BF16),
-            V((2, NQ, HALF), BF16), V((NSH, 8, 128), F32), V((NSH, 8, 128), F32),
+            V((NSU, 16, 256), BF16), V((NSU, 16, 128), F32), V((16, D), F32), V((4, 16, QW), BF16),
+            V((4, NQ, QW), BF16), V((NSH, 8, 128), F32), V((NSH, 8, 128), F32),
             V((D, NQ), F32), V((D, NQ), F32),
             V((8, 256), F32), V((NSU, 8, 256), F32), V((8, 256), F32), V((NSH, 8, 256), F32),
             V((NQ, 128), F32), V((NQ, D), F32), V((NQ, D), F32), V((2 * NQ, D), BF16),
             V((CHUNKS, 2, NSH, 8, CW), F32), V((CHUNKS, NSH, 8, CW), F32), V((CHUNKS, NSH, 8, CW), F32),
             V((CHUNKS, 4, 8, CW), F32),
-            V((4, 8, CW), F32), V((4, 8, CW), F32), V((2, 8, 128), F32), V((NSH, 8, 128), F32),
+            V((4, 16, CW), F32), V((4, 16, CW), F32), V((NSH, 8, 128), F32), V((NSH, 8, 128), F32), V((2, 8, 128), F32), V((NSH, 8, 128), F32),
             V((NSU, 24, 128), F32), V((NSU, 24, 128), F32),
             DMA(()), DMA((2,)),
             DMA((NSU,)), DMA((NSU,)), DMA((NSU,)), DMA((NSU,)),
-            DMA((4,)), DMA((4,)), DMA((4, 4)), DMA((4, 4)), DMA((NSH,)), DMA((NSH,)), DMA(()), DMA(()),
+            DMA((4,)), DMA((4,)), DMA((4, 4)), DMA((4, 4)), DMA((NSH,)), DMA((NSH,)), DMA((2,)), DMA((2,)),
             DMA((NSU,)), DMA((NSU,)), DMA((NSH,)), DMA((NSH,)),
             DMA((NSH,)), DMA((NSH,)), DMA((NSU,)), DMA((NSU,)),
             DMA((CHUNKS,)), DMA((CHUNKS,)), DMA((CHUNKS, 4)), DMA((CHUNKS, 4)), DMA((CHUNKS, 4)), DMA((CHUNKS, 4)),
-            DMA((4,)), DMA((4,)),
+            DMA((4,)), DMA((4,)), DMA((NSH,)), DMA((NSH,)),
         ],
         compiler_params=pltpu.CompilerParams(
             collective_id=0, has_side_effects=True, vmem_limit_bytes=50 * 1024 * 1024

time: 64.9 us -> 62 us (0.955)
  Pallas kernels: 61 us -> 58.1 us
    pallas_call x1, Pallas kernels: 61 us -> 58.1 us  [shards(): pl.pallas_call(kernel, name='retrieve', out_shape=(jax.ShapeDtypeStruct((...]
where the time goes in v3:
time: 62 us; the launch traced here: 61.8 us
  Pallas kernels  58.1 us (94%)
  local copies, waits for them, and re-layouts  3.06 us (5%)
  between operations  0.65 us (1%)
    pallas_call x1, Pallas kernels, shards(): pl.pallas_call(kernel, name='retrieve', out_shape=(jax.ShapeDtypeStruct((...  58.1 us
    unnamed x7, local copies, waits for them, and re-layouts  3.06 us

profile of v3, /device:TPU:0, one launch (start us, length us, event | category | flops | bytes accessed | tf_op | source)
XLA Modules:
  0.0 61.8 jit_solution(2756234271532878471)
XLA Ops:
  0.6 0.0 copy-start
  0.6 0.7 %copy-done = bf16[2,2048]{1,0:T(2,128)(2,1)S(1)} copy-done((bf16[2,2048]{1,0:T(2,128)(2,1)S(1)}, bf16[2,2048]{1,0:T(2,128)(2,1)}, u32[]{:S(2)}) %copy-start) | copy-done | bytes 8216
  1.3 0.0 copy-start.1
  1.3 0.7 %copy-done.1 = s32[2,200]{1,0:T(2,128)S(1)} copy-done((s32[2,200]{1,0:T(2,128)S(1)}, s32[2,200]{1,0:T(2,128)}, u32[]{:S(2)}) %copy-start.1) | copy-done | bytes 1624
  2.0 58.1 %retrieve.1 = (f32[1,2]{1,0:T(1,128)S(1)}, f32[2,200]{1,0:T(2,128)S(1)}, bf16[2,2048]{1,0:T(2,128)(2,1)S(1)}) custom-call(s32[2,200]{1,0:T(2,128)S(1)} %copy-done.1, bf16[2,2048]{1,0:T(2,128)(2,1)S(1)} %copy-done, bf16[2048,2048]{1,0:T(8,128)(2,1)} %p_hbm.1), custom_call_target="tpu_custom_call" | custom-call | tf_op jit(solution)/shard_map/retrieve/pallas_call | solution.py:472
  60.1 0.5 copy.9
  60.6 0.6 copy.10
  61.2 0.6 copy.11
Async XLA Ops:
  0.6 0.7 %copy-start = (bf16[2,2048]{1,0:T(2,128)(2,1)S(1)}, bf16[2,2048]{1,0:T(2,128)(2,1)}, u32[]{:S(2)}) copy-start(bf16[2,2048]{1,0:T(2,128)(2,1)} %q_hbm.1) | copy-start | bytes 24580
  1.3 0.7 %copy-start.1 = (s32[2,200]{1,0:T(2,128)S(1)}, s32[2,200]{1,0:T(2,128)}, u32[]{:S(2)}) copy-start(s32[2,200]{1,0:T(2,128)} %cand_hbm.1) | copy-start | bytes 4804

commit v4 on v3

--- a/solution.py
+++ b/solution.py
@@ -58,8 +58,10 @@
         pl.semaphore_signal(barrier, inc=1, device_id=sub_peer(k), device_id_type=MESH)
         return c
 
-    lax.fori_loop(1, NSH, greet, 0)
-    lax.fori_loop(1, NSU, greet_sub, 0)
+    for k in (8, 2, 4, 12, 1, 3):
+        greet(k, 0)
+    for k in (4, 5, 2, 3, 6, 7, 1):
+        greet_sub(k, 0)
     load_p = pltpu.make_async_copy(p_hbm, p_v, p_sem)
     load_p.start()
 
@@ -77,7 +79,7 @@
     qsend[...] = qf[...].astype(BF16)
     qbuf[su] = qsend[...]
 
-    pl.semaphore_wait(barrier, NSH - 1 + NSU - 1)
+    pl.semaphore_wait(barrier, 6 + 7)
 
     def d_q1(k):
         return remote(qsend, qbuf.at[su], q1s.at[k], q1r.at[k], sub_peer(k))
@@ -138,10 +140,6 @@
 
     loop(4, lambda k: d_q2(k).start())
     loop(4, lambda k: d_q3(0, k).start())
-    for j in range(1, 4):
-        d_q2(j).wait()
-        loop(4, lambda k: d_q3(j, k).start())
-
     loop(NSU, lambda k: d_c1(k).wait())
     lane = iota((8, 128), 1)
     base = (sh % 8) * 16
@@ -155,6 +153,11 @@
     for j in range(NSH):
         ctile[j] = tiles[j]
     crecv[sh] = ctile[sh]
+
+    for j in range(1, 4):
+        d_q2(j).wait()
+        loop(4, lambda k: d_q3(j, k).start())
+
     loop(NSH, lambda k: d_c2(k).start())
     for j in range(4):
         loop(4, lambda k: d_q3(j, k).wait())
@@ -210,9 +213,15 @@
     masked = jnp.where(valid, scores, NEG)
     m0 = jnp.max(masked, axis=0, keepdims=True)
     l0 = jnp.sum(jnp.where(valid, jnp.exp(masked - m0), 0.0), axis=0, keepdims=True)
-    stat1[0:1, :] = m0
-    stat1[1:2, :] = l0
-    stat1[2:8, :] = jnp.zeros((6, 256), F32)
+    def fold(v):
+        return jnp.concatenate([v[:, 0:128], v[:, 128:256]], axis=0)
+
+    def unfold(v):
+        return jnp.concatenate([v[0:1, :], v[1:2, :]], axis=1)
+
+    stat1[0:2, :] = fold(m0)
+    stat1[2:4, :] = fold(l0)
+    stat1[4:8, :] = jnp.zeros((4, 128), F32)
     stat1r[su] = stat1[...]
 
     def d_s1(k):
@@ -242,20 +251,19 @@
     loop(NSU, lambda k: d_s1(k).wait())
 
     def join(buf, n, row):
-        top = buf[0, row:row + 1, :]
+        top = buf[0, row:row + 2, :]
         for i in range(1, n):
-            top = jnp.maximum(top, buf[i, row:row + 1, :])
-        total = jnp.zeros((1, 256), F32)
+            top = jnp.maximum(top, buf[i, row:row + 2, :])
+        total = jnp.zeros((2, 128), F32)
         for i in range(n):
-            total = total + buf[i, row + 1:row + 2, :] * jnp.exp(buf[i, row:row + 1, :] - top)
+            total = total + buf[i, row + 2:row + 4, :] * jnp.exp(buf[i, row:row + 2, :] - top)
         return top, total
 
     m1, l1 = join(stat1r, NSU, 0)
-    stat2[0:1, :] = m1
-    stat2[1:2, :] = l1
-    stat2[2:3, :] = cm
-    stat2[3:4, :] = cl
-    stat2[4:8, :] = jnp.zeros((4, 256), F32)
+    stat2[0:2, :] = m1
+    stat2[2:4, :] = l1
+    stat2[4:6, :] = fold(cm)
+    stat2[6:8, :] = fold(cl)
     stat2r[sh] = stat2[...]
 
     def d_s2(k):
@@ -294,8 +302,8 @@
 
     lax.fori_loop(0, NQ // 16, tally, 0)
     loop(NSH, lambda k: d_s2(k).wait())
-    m2, l2 = join(stat2r, NSH, 0)
-    cm2, cl2 = join(stat2r, NSH, 2)
+    m2, l2 = (unfold(v) for v in join(stat2r, NSH, 0))
+    cm2, cl2 = join(stat2r, NSH, 4)
 
     scale = jnp.exp(m0 - m2) / l2
     probs = jnp.where(valid, jnp.exp(masked - m0), 0.0) * scale
@@ -394,8 +402,7 @@
             for t in range(2):
                 col = (d % 2) * 8 + t * 4 + d // 2
                 outs[d][t] = jnp.where(here, jnp.broadcast_to(mine[:, col:col + 1], (8, 128)), outs[d][t])
-    coarse = jnp.concatenate([cm2[:, 0:128], cm2[:, 128:256], cl2[:, 0:128], cl2[:, 128:256],
-                              jnp.zeros((4, 128), F32)], axis=0)
+    coarse = jnp.concatenate([cm2, cl2, jnp.zeros((4, 128), F32)], axis=0)
     for d in range(NSU):
         for t in range(2):
             pusend[d, t * 8:t * 8 + 8, :] = outs[d][t]
@@ -484,7 +491,7 @@
             V((NSU, 16, 256), BF16), V((NSU, 16, 128), F32), V((16, D), F32), V((4, 16, QW), BF16),
             V((4, NQ, QW), BF16), V((NSH, 8, 128), F32), V((NSH, 8, 128), F32),
             V((D, NQ), F32), V((D, NQ), F32),
-            V((8, 256), F32), V((NSU, 8, 256), F32), V((8, 256), F32), V((NSH, 8, 256), F32),
+            V((8, 128), F32), V((NSU, 8, 128), F32), V((8, 128), F32), V((NSH, 8, 128), F32),
             V((NQ, 128), F32), V((NQ, D), F32), V((NQ, D), F32), V((2 * NQ, D), BF16),
             V((CHUNKS, 2, NSH, 8, CW), F32), V((CHUNKS, NSH, 8, CW), F32), V((CHUNKS, NSH, 8, CW), F32),
             V((CHUNKS, 4, 8, CW), F32),

time: 62 us -> 60.5 us (0.976)
  Pallas kernels: 58.1 us -> 56.6 us
    pallas_call x1, Pallas kernels: 58.1 us -> 56.6 us  [shards(): pl.pallas_call(kernel, name='retrieve', out_shape=(jax.ShapeDtypeStruct((...]
where the time goes in v4:
time: 60.5 us; the launch traced here: 60.3 us
  Pallas kernels  56.6 us (94%)
  local copies, waits for them, and re-layouts  3.06 us (5%)
  between operations  0.65 us (1%)
    pallas_call x1, Pallas kernels, shards(): pl.pallas_call(kernel, name='retrieve', out_shape=(jax.ShapeDtypeStruct((...  56.6 us
    unnamed x7, local copies, waits for them, and re-layouts  3.06 us

profile of v4, /device:TPU:0, one launch (start us, length us, event | category | flops | bytes accessed | tf_op | source)
XLA Modules:
  0.0 60.3 jit_solution(4662506688319180902)
XLA Ops:
  0.6 0.0 copy-start
  0.6 0.7 %copy-done = bf16[2,2048]{1,0:T(2,128)(2,1)S(1)} copy-done((bf16[2,2048]{1,0:T(2,128)(2,1)S(1)}, bf16[2,2048]{1,0:T(2,128)(2,1)}, u32[]{:S(2)}) %copy-start) | copy-done | bytes 8216
  1.3 0.0 copy-start.1
  1.3 0.7 %copy-done.1 = s32[2,200]{1,0:T(2,128)S(1)} copy-done((s32[2,200]{1,0:T(2,128)S(1)}, s32[2,200]{1,0:T(2,128)}, u32[]{:S(2)}) %copy-start.1) | copy-done | bytes 1624
  2.0 56.6 %retrieve.1 = (f32[1,2]{1,0:T(1,128)S(1)}, f32[2,200]{1,0:T(2,128)S(1)}, bf16[2,2048]{1,0:T(2,128)(2,1)S(1)}) custom-call(s32[2,200]{1,0:T(2,128)S(1)} %copy-done.1, bf16[2,2048]{1,0:T(2,128)(2,1)S(1)} %copy-done, bf16[2048,2048]{1,0:T(8,128)(2,1)} %p_hbm.1), custom_call_target="tpu_custom_call" | custom-call | tf_op jit(solution)/shard_map/retrieve/pallas_call | solution.py:479
  58.7 0.5 copy.9
  59.2 0.6 copy.10
  59.7 0.6 copy.11
Async XLA Ops:
  0.6 0.7 %copy-start = (bf16[2,2048]{1,0:T(2,128)(2,1)S(1)}, bf16[2,2048]{1,0:T(2,128)(2,1)}, u32[]{:S(2)}) copy-start(bf16[2,2048]{1,0:T(2,128)(2,1)} %q_hbm.1) | copy-start | bytes 24580
  1.3 0.7 %copy-start.1 = (s32[2,200]{1,0:T(2,128)S(1)}, s32[2,200]{1,0:T(2,128)}, u32[]{:S(2)}) copy-start(s32[2,200]{1,0:T(2,128)} %cand_hbm.1) | copy-start | bytes 4804

commit v5 on v4

--- a/solution.py
+++ b/solution.py
@@ -9,14 +9,14 @@
 NDEV = NSH * NSU
 D = 2048
 QW = D // 4
-LAST = 256
+LAST = 512
 PREFIX = 64
 CANDS = 200
 CAP = 8
 NQ = 256
 CHUNKS = 4
 CW = D // CHUNKS
-TWO_HOP = CHUNKS - 1
+TWO_HOP = CHUNKS - 2
 NEG = -3.0e38
 MESH = pl.DeviceIdType.MESH
 F32, BF16, I32 = jnp.float32, jnp.bfloat16, jnp.int32
@@ -174,16 +174,16 @@
         return dot_nt(p_v[rows, cols], qall[h])
 
     def score_half(i, c):
-        rows = pl.ds(pl.multiple_of(i * 512, 512), 512)
+        rows = pl.ds(pl.multiple_of(i * 1024, 1024), 1024)
         st[rows, :] = score(core * 2, rows) + score(core * 2 + 1, rows)
         return c
 
     def score_third(i, c):
-        rows = pl.ds(pl.multiple_of(i * 512, 512), 512)
+        rows = pl.ds(pl.multiple_of(i * 1024, 1024), 1024)
         st[rows, :] = st[rows, :] + score((1 - core) * 2, rows)
         return c
 
-    lax.fori_loop(0, D // 512, score_half, 0)
+    lax.fori_loop(0, D // 1024, score_half, 0)
     loop(NSH, lambda k: d_c2(k).wait())
     first, second_ = crecv[0], crecv[8]
     for i in range(1, 8):
@@ -194,7 +194,7 @@
     rows_of = [jnp.broadcast_to(codes[s:s + 1, :], (8, 256)) for s in range(CAP)]
     sub_iota = iota((8, 256), 0)
     d_sib(0).wait()
-    lax.fori_loop(0, D // 512, score_third, 0)
+    lax.fori_loop(0, D // 1024, score_third, 0)
     d_sib(1).wait()
 
     def score_last(i, accs):
@@ -414,13 +414,8 @@
 
     loop(NSU, lambda k: d_pu(k).start())
 
-    second(2)
     third(0)
     third(1)
-    at_once(3)
-    lrecv[a2 * 4 + z] = lsend[a2 * 4 + z]
-    loop(NSH, lambda k: d_l(k).start())
-    third(2)
     for i in range(4):
         zsend[i, TWO_HOP:8, :] = jnp.zeros((8 - TWO_HOP, CW), F32)
         zsend[i, 8 + TWO_HOP:16, :] = jnp.zeros((8 - TWO_HOP, CW), F32)
@@ -430,6 +425,10 @@
         return remote(zsend.at[z ^ k], zr.at[z], zs_.at[k], zr_.at[k], sub_peer(2 * k))
 
     loop(4, lambda k: d_z(k).start())
+    at_once(2)
+    at_once(3)
+    lrecv[a2 * 4 + z] = lsend[a2 * 4 + z]
+    loop(NSH, lambda k: d_l(k).start())
 
     loop(NSU, lambda k: d_pu(k).wait())
     for t in range(2):
@@ -495,7 +494,7 @@
             V((NQ, 128), F32), V((NQ, D), F32), V((NQ, D), F32), V((2 * NQ, D), BF16),
             V((CHUNKS, 2, NSH, 8, CW), F32), V((CHUNKS, NSH, 8, CW), F32), V((CHUNKS, NSH, 8, CW), F32),
             V((CHUNKS, 4, 8, CW), F32),
-            V((4, 16, CW), F32), V((4, 16, CW), F32), V((NSH, 8, 128), F32), V((NSH, 8, 128), F32), V((2, 8, 128), F32), V((NSH, 8, 128), F32),
+            V((4, 16, CW), F32), V((4, 16, CW), F32), V((NSH, 16, 128), F32), V((NSH, 16, 128), F32), V((2, 8, 128), F32), V((NSH, 8, 128), F32),
             V((NSU, 24, 128), F32), V((NSU, 24, 128), F32),
             DMA(()), DMA((2,)),
             DMA((NSU,)), DMA((NSU,)), DMA((NSU,)), DMA((NSU,)),

time: 60.5 us -> 58.8 us (0.972)
  Pallas kernels: 56.6 us -> 54.9 us
    pallas_call x1, Pallas kernels: 56.6 us -> 54.9 us  [shards(): pl.pallas_call(kernel, name='retrieve', out_shape=(jax.ShapeDtypeStruct((...]
where the time goes in v5:
time: 58.8 us; the launch traced here: 58.6 us
  Pallas kernels  54.9 us (93%)
  local copies, waits for them, and re-layouts  3.06 us (5%)
  between operations  0.65 us (1%)
    pallas_call x1, Pallas kernels, shards(): pl.pallas_call(kernel, name='retrieve', out_shape=(jax.ShapeDtypeStruct((...  54.9 us
    unnamed x7, local copies, waits for them, and re-layouts  3.06 us

profile of v5, /device:TPU:0, one launch (start us, length us, event | category | flops | bytes accessed | tf_op | source)
XLA Modules:
  0.0 58.6 jit_solution(1693665627563630104)
XLA Ops:
  0.6 0.0 copy-start
  0.6 0.7 %copy-done = bf16[2,2048]{1,0:T(2,128)(2,1)S(1)} copy-done((bf16[2,2048]{1,0:T(2,128)(2,1)S(1)}, bf16[2,2048]{1,0:T(2,128)(2,1)}, u32[]{:S(2)}) %copy-start) | copy-done | bytes 8216
  1.3 0.0 copy-start.1
  1.3 0.7 %copy-done.1 = s32[2,200]{1,0:T(2,128)S(1)} copy-done((s32[2,200]{1,0:T(2,128)S(1)}, s32[2,200]{1,0:T(2,128)}, u32[]{:S(2)}) %copy-start.1) | copy-done | bytes 1624
  2.0 54.9 %retrieve.1 = (f32[1,2]{1,0:T(1,128)S(1)}, f32[2,200]{1,0:T(2,128)S(1)}, bf16[2,2048]{1,0:T(2,128)(2,1)S(1)}) custom-call(s32[2,200]{1,0:T(2,128)S(1)} %copy-done.1, bf16[2,2048]{1,0:T(2,128)(2,1)S(1)} %copy-done, bf16[2048,2048]{1,0:T(8,128)(2,1)} %p_hbm.1), custom_call_target="tpu_custom_call" | custom-call | tf_op jit(solution)/shard_map/retrieve/pallas_call | solution.py:478
  56.9 0.5 copy.9
  57.5 0.6 copy.10
  58.0 0.6 %copy.11 = bf16[2,2048]{1,0:T(2,128)(2,1)} copy(bf16[2,2048]{1,0:T(2,128)(2,1)S(1)} %get-tuple-element.14) | data formatting | bytes 16384
Async XLA Ops:
  0.6 0.7 %copy-start = (bf16[2,2048]{1,0:T(2,128)(2,1)S(1)}, bf16[2,2048]{1,0:T(2,128)(2,1)}, u32[]{:S(2)}) copy-start(bf16[2,2048]{1,0:T(2,128)(2,1)} %q_hbm.1) | copy-start | bytes 24580
  1.3 0.7 %copy-start.1 = (s32[2,200]{1,0:T(2,128)S(1)}, s32[2,200]{1,0:T(2,128)}, u32[]{:S(2)}) copy-start(s32[2,200]{1,0:T(2,128)} %cand_hbm.1) | copy-start | bytes 4804

commit v6 on v5

--- a/solution.py
+++ b/solution.py
@@ -9,7 +9,7 @@
 NDEV = NSH * NSU
 D = 2048
 QW = D // 4
-LAST = 512
+LAST = 1024
 PREFIX = 64
 CANDS = 200
 CAP = 8

time: 58.8 us -> 58.5 us (level)
  no operation moved by 1% of the time
where the time goes in v6:
time: 58.5 us; the launch traced here: 58.3 us
  Pallas kernels  54.6 us (93%)
  local copies, waits for them, and re-layouts  3.06 us (5%)
  between operations  0.65 us (1%)
    pallas_call x1, Pallas kernels, shards(): pl.pallas_call(kernel, name='retrieve', out_shape=(jax.ShapeDtypeStruct((...  54.6 us
    unnamed x7, local copies, waits for them, and re-layouts  3.06 us

profile of v6, /device:TPU:0, one launch (start us, length us, event | category | flops | bytes accessed | tf_op | source)
XLA Modules:
  0.0 58.3 jit_solution(8448202546829979588)
XLA Ops:
  0.6 0.0 copy-start
  0.6 0.7 %copy-done = bf16[2,2048]{1,0:T(2,128)(2,1)S(1)} copy-done((bf16[2,2048]{1,0:T(2,128)(2,1)S(1)}, bf16[2,2048]{1,0:T(2,128)(2,1)}, u32[]{:S(2)}) %copy-start) | copy-done | bytes 8216
  1.3 0.0 copy-start.1
  1.3 0.7 %copy-done.1 = s32[2,200]{1,0:T(2,128)S(1)} copy-done((s32[2,200]{1,0:T(2,128)S(1)}, s32[2,200]{1,0:T(2,128)}, u32[]{:S(2)}) %copy-start.1) | copy-done | bytes 1624
  2.0 54.6 %retrieve.1 = (f32[1,2]{1,0:T(1,128)S(1)}, f32[2,200]{1,0:T(2,128)S(1)}, bf16[2,2048]{1,0:T(2,128)(2,1)S(1)}) custom-call(s32[2,200]{1,0:T(2,128)S(1)} %copy-done.1, bf16[2,2048]{1,0:T(2,128)(2,1)S(1)} %copy-done, bf16[2048,2048]{1,0:T(8,128)(2,1)} %p_hbm.1), custom_call_target="tpu_custom_call" | custom-call | tf_op jit(solution)/shard_map/retrieve/pallas_call | solution.py:478
  56.6 0.5 copy.9
  57.1 0.6 copy.10
  57.7 0.6 %copy.11 = bf16[2,2048]{1,0:T(2,128)(2,1)} copy(bf16[2,2048]{1,0:T(2,128)(2,1)S(1)} %get-tuple-element.14) | data formatting | bytes 16384
Async XLA Ops:
  0.6 0.7 %copy-start = (bf16[2,2048]{1,0:T(2,128)(2,1)S(1)}, bf16[2,2048]{1,0:T(2,128)(2,1)}, u32[]{:S(2)}) copy-start(bf16[2,2048]{1,0:T(2,128)(2,1)} %q_hbm.1) | copy-start | bytes 24580
  1.3 0.7 %copy-start.1 = (s32[2,200]{1,0:T(2,128)S(1)}, s32[2,200]{1,0:T(2,128)}, u32[]{:S(2)}) copy-start(s32[2,200]{1,0:T(2,128)} %cand_hbm.1) | copy-start | bytes 4804
